TPU v7x, 32 devices: a whole 2x2x4 slice. The times are simulated.
32 devices in a mesh: seq: 8 (over z, x), head: 2 (over y), pair: 2 (over core).
Axes of the slice: x: 2, y: 2, z: 4, core: 2. Of those that a mesh axis runs over, the one named last changes fastest.
Arguments:
- queries: bfloat16 [6144, 5120], P(('pair', 'seq'), 'head'), parts along dimension 0, may hold values from -12 to 12
- keys: bfloat16 [6144, 5120], P(('pair', 'seq'), 'head'), parts along dimension 0, may hold values from -12 to 12
- values: bfloat16 [6144, 5120], P(('pair', 'seq'), 'head'), parts along dimension 0, may hold values from -6 to 6
- cross_query: bfloat16 [6144, 5120], P(('pair', 'seq'), 'head'), parts along dimension 0, may hold values from -12 to 12
- text_keys: bfloat16 [1024, 5120], P('pair', 'head'), parts along dimension 0, may hold values from -12 to 12
- text_values: bfloat16 [1024, 5120], P('pair', 'head'), parts along dimension 0, may hold values from -6 to 6
- out_weight: bfloat16 [5120, 5120], P('head'), may hold values from -0.078125 to 0.078125
- block_list: int32 [24, 18], replicated, may hold values from 0 to 23, as said below
- block_count: int32 [24], replicated, may hold values from 6 to 18, as said below
Outputs:
- block_stream: bfloat16 [6144, 5120], P(('pair', 'seq'), 'head'), parts along dimension 0
- cross_heads: bfloat16 [6144, 5120], P(('pair', 'seq'), 'head'), parts along dimension 0
There are 2 independent parts, one for each index of `pair`. A program takes and returns all parts, laid end to end along the dimension named above; an argument that names none is the same for every part. Nothing has to cross between parts.
Inputs may be any that keep to these rules, and one draw needn't show every extreme that they name: `block_list`: each row holds 18 distinct key blocks; its first block_count entries include every block of frame groups f - 1, f and f + 1 (those that exist) and of group 0, with f = row // 3 and a frame group being 3 consecutive blocks. `block_count`: some row uses all 18 entries.
All inputs are finite; a program needn't handle non-finite values.
Results may differ from a plain program's by a relative error of at most 0.029.
Values may be sent and summed in bfloat16 or wider, within the bound.
A program may use at most 192 MiB of HBM per device.

v0:
```python
import jax
import jax.numpy as jnp
from jax import lax
from jax.sharding import PartitionSpec as P

DH = 128
BLK = 128


def allowed_table(block_list, block_count):
    slots = jnp.arange(block_list.shape[1], dtype=jnp.int32)
    targets = jnp.arange(block_list.shape[0], dtype=jnp.int32)
    hit = (block_list[:, :, None] == targets[None, None, :]) & (
        slots[None, :, None] < block_count[:, None, None]
    )
    return jnp.any(hit, axis=1).astype(jnp.int32)


def attend_tile(carry, query_three, key_tile, value_tile, tile_mask, scale):
    row_max, total, summed = carry
    count = key_tile.shape[0]
    heads_here = query_three.shape[1]
    key_three = key_tile.reshape(count, heads_here, DH)
    value_three = value_tile.reshape(count, heads_here, DH)
    score = (
        jnp.einsum("qhd,khd->hqk", query_three, key_three, preferred_element_type=jnp.float32)
        * scale
    )
    score = jnp.where(tile_mask[None], score, -1e30)
    new_max = jnp.maximum(row_max, jnp.max(score, axis=2))
    weight = jnp.where(tile_mask[None], jnp.exp(score - new_max[:, :, None]), 0.0)
    factor = jnp.exp(row_max - new_max)
    total = total * factor + jnp.sum(weight, axis=2)
    update = jnp.einsum(
        "hqk,khd->hqd", weight.astype(jnp.bfloat16), value_three, preferred_element_type=jnp.float32
    )
    summed = summed * factor[:, :, None] + update
    return (new_max, total, summed)


def masked_update(carry, query_three, key_tile, value_tile, tile_mask, scale):
    return attend_tile(carry, query_three, key_tile, value_tile, tile_mask, scale)


def empty_state(heads_here, count):
    return (
        jnp.full((heads_here, count), -1e30, jnp.float32),
        jnp.zeros((heads_here, count), jnp.float32),
        jnp.zeros((heads_here, count, DH), jnp.float32),
    )


def body(
    queries, keys, values, cross_query, text_keys, text_values, out_weight, block_list, block_count
):
    scale = DH ** (-0.5)
    rows = queries.shape[0]
    heads_here = queries.shape[1] // DH
    blocks_here = rows // BLK
    allowed = allowed_table(block_list, block_count) > 0
    my_first = lax.axis_index("seq") * blocks_here
    query_three = queries.reshape(rows, heads_here, DH)
    row_allowed = jnp.repeat(
        lax.dynamic_slice_in_dim(allowed, my_first, blocks_here, 0), BLK, axis=0
    )
    key_piece = lax.all_gather(keys, "seq", axis=0, tiled=True)
    value_piece = lax.all_gather(values, "seq", axis=0, tiled=True)
    count = key_piece.shape[0]
    shards_in = count // rows
    factor = 1
    for candidate in range(1, shards_in + 1):
        if shards_in % candidate == 0 and candidate * rows <= 1536:
            factor = candidate
    width = factor * rows
    piece_mask = jnp.repeat(row_allowed, BLK, axis=1)
    tiles = count // width
    key_tiles = key_piece.reshape(tiles, width, key_piece.shape[1])
    value_tiles = value_piece.reshape(tiles, width, value_piece.shape[1])
    mask_tiles = piece_mask.reshape(rows, tiles, width).transpose(1, 0, 2)

    def step(state, items):
        return (masked_update(state, query_three, items[0], items[1], items[2], scale), None)

    state, unused = lax.scan(
        step, empty_state(heads_here, rows), (key_tiles, value_tiles, mask_tiles)
    )
    row_max, total, summed = state
    self_three = (summed / total[:, :, None]).transpose(1, 0, 2)
    self_heads = self_three.reshape(rows, heads_here * DH).astype(jnp.bfloat16)
    term = jnp.dot(self_heads, out_weight, preferred_element_type=jnp.float32)
    block_stream = lax.psum_scatter(
        term.astype(jnp.bfloat16), "head", scatter_dimension=1, tiled=True
    )
    cross_three = cross_query.reshape(rows, heads_here, DH)
    text_count = text_keys.shape[0]
    text_key_three = text_keys.reshape(text_count, heads_here, DH)
    text_value_three = text_values.reshape(text_count, heads_here, DH)
    cross_score = (
        jnp.einsum("qhd,khd->hqk", cross_three, text_key_three, preferred_element_type=jnp.float32)
        * scale
    )
    cross_max = jnp.max(cross_score, axis=2, keepdims=True)
    cross_weight = jnp.exp(cross_score - cross_max)
    cross_total = jnp.sum(cross_weight, axis=2)
    cross_sum = jnp.einsum(
        "hqk,khd->hqd",
        cross_weight.astype(jnp.bfloat16),
        text_value_three,
        preferred_element_type=jnp.float32,
    )
    cross_heads = (
        (cross_sum / cross_total[:, :, None])
        .transpose(1, 0, 2)
        .reshape(rows, heads_here * DH)
        .astype(jnp.bfloat16)
    )
    return (block_stream, cross_heads)


def solution(mesh):
    in_specs = (
        P(("pair", "seq"), "head"),
        P(("pair", "seq"), "head"),
        P(("pair", "seq"), "head"),
        P(("pair", "seq"), "head"),
        P("pair", "head"),
        P("pair", "head"),
        P("head", None),
        P(),
        P(),
    )
    out_specs = (P(("pair", "seq"), "head"), P(("pair", "seq"), "head"))
    return jax.shard_map(body, mesh=mesh, in_specs=in_specs, out_specs=out_specs, check_vma=False)
```

profile of v0, /device:TPU:0, one launch (start us, length us, event | category | flops | bytes accessed | tf_op | source)
XLA Modules:
  0.0 726.6 jit_solution(5979538835152849223)
XLA Ops:
  7.2 0.0 all-gather.3.cloned.1.call-start
  7.2 0.7 all-gather.3.cloned.1.call-update
  7.9 0.0 all-gather.5.cloned.1.call-start
  7.9 0.7 all-gather.5.cloned.1.call-update
  8.6 0.0 reduce-scatter.2.cloned.1.call-start
  8.7 0.8 copy.45
  9.5 0.7 iota_compare_fusion.1
  10.2 0.2 fusion.23
  10.4 0.1 copy.46
  10.5 0.1 broadcast_in_dim.49
  10.6 4.0 copy.47
  14.6 2.8 copy.49
  17.4 210.3 %all-gather.3.cloned.1.call-done = bf16[3072,2560]{1,0:T(8,128)(2,1)} async-done(((bf16[384,2560]{1,0:T(8,128)(2,1)}), bf16[3072,2560]{1,0:T(8,128)(2,1)}) %all-gather.3.cloned.1.call-update) | async-done | bytes 15728656 | tf_op jit(solution)/shard_map/all_gather | solution.py:66
  227.7 215.2 %all-gather.5.cloned.1.call-done = bf16[3072,2560]{1,0:T(8,128)(2,1)} async-done(((bf16[384,2560]{1,0:T(8,128)(2,1)}), bf16[3072,2560]{1,0:T(8,128)(2,1)}) %all-gather.5.cloned.1.call-update) | async-done | bytes 15728656 | tf_op jit(solution)/shard_map/all_gather | solution.py:67
  442.9 1.3 broadcast_in_dim.50
  444.2 200.3 %while.15 = (s32[]{:T(128)}, f32[20,384]{1,0:T(8,128)S(1)}, f32[20,384]{1,0:T(8,128)S(1)}, f32[20,384,128]{2,1,0:T(8,128)}, pred[2,384,1536]{1,2,0:T(8,128)(4,1)...) while((s32[]{:T(128)}, f32[20,384]{1,0:T(8,128)S(1)}, ...), condition=%wide.region_4.5_spmd.clone, body=%wide.region_1.4_spmd.clone.sunk | while | flops 6196139520 | bytes 233472128 | solution.py:84
  444.2 10.9 %constant_dynamic-slice_fusion.3 = (bf16[1,1536,2560]{2,1,0:T(8,128)(2,1)}, bf16[1,1536,2560]{2,1,0:T(8,128)(2,1)}) fusion(bf16[2,1536,2560]{2,1,0:T(8,128)(2,1)} %get-tuple-element.218, s32[]{:T(128)} %get-tuple-element.201, bf16[2,1536,2560]{2,1,0:T(8,128)(2,1)} %get-tuple-element.216), kind=kLoop, calls=%fused_computation.14.clone.1 | loop fusion | bytes 31457284 | tf_op jit(solution)/shard_map/while/body/jit(dynamic_index_in_dim)/dynamic_slice | solution.py:84
  455.2 10.6 %copy.70 = bf16[1,1536,2560]{1,2,0:T(8,128)(2,1)} copy(bf16[1,1536,2560]{2,1,0:T(8,128)(2,1)} %get-tuple-element.185) | data formatting | bytes 15728640 | tf_op jit(solution)/shard_map/while/body/jit(dynamic_index_in_dim)/dynamic_slice | solution.py:84
  465.8 1.3 dynamic-slice_bitcast_fusion.2
  467.0 20.6 %fusion.45 = (f32[20,384]{1,0:T(8,128)S(1)}, f32[20,1536,384]{2,1,0:T(8,128)}) fusion(pred[384,1536]{0,1:T(8,128)(4,1)S(1)} %dynamic-slice_bitcast_fusion.2, bf16[1536,20,128]{0,2,1:T(8,128)(2,1)} %bitcast.67, bf16[384,20,128]{2,0,1:T(8,128)(2,1)S(1)} %get-tuple-element.217), kind=kOutput, calls=%fused_computation.2.clone.1 | convolution fusion | flops 3055280640 | bytes 57636864 | tf_op jit(solution)/shard_map/while/body/eval_jaxpr/qhd,khd->hqk/dot_general | solution.py:26
  487.7 20.8 %fusion.46 = f32[20,384]{1,0:T(8,128)S(1)} fusion(f32[20,1536,384]{2,1,0:T(8,128)} %get-tuple-element.187, f32[20,384]{1,0:T(8,128)S(1)} %select_maximum_fusion.2, pred[384,1536]{0,1:T(8,128)(4,1)S(1)} %dynamic-slice_bitcast_fusion.2), kind=kLoop, calls=%fused_computation.4.clone.1 | loop fusion | flops 58974720 | bytes 47837184 | tf_op jit(solution)/shard_map/while/body/eval_jaxpr/reduce_sum | solution.py:33
  508.5 10.6 %copy.71 = bf16[1,1536,2560]{1,2,0:T(8,128)(2,1)} copy(bf16[1,1536,2560]{2,1,0:T(8,128)(2,1)} %get-tuple-element.189) | data formatting | bytes 15728640 | tf_op jit(solution)/shard_map/while/body/jit(dynamic_index_in_dim)/dynamic_slice | solution.py:84
  519.2 24.9 %fusion.48 = f32[20,384,128]{2,1,0:T(8,128)} fusion(f32[20,384,128]{2,1,0:T(8,128)} %get-tuple-element.204, bf16[1536,20,128]{0,2,1:T(8,128)(2,1)} %bitcast.68, f32[20,1536,384]{2,1,0:T(8,128)} %get-tuple-element.187, f32[20,384]{1,0:T(8,128)S(1)} %select_maximum_fusion.2, pred[384,1536]{0,1:T(8,128)(4,1)S(1)} %dynamic-slice_bitcast_fusion.2, ...), kind=kOutput, calls=%fused_computation.8.clone.1 | convolution fusion | flops 3081830400 | bytes 63565824 | tf_op jit(solution)/shard_map/while/body/eval_jaxpr/hqk,khd->hqd/dot_general | solution.py:34
  544.1 10.9 %constant_dynamic-slice_fusion.3 = (bf16[1,1536,2560]{2,1,0:T(8,128)(2,1)}, bf16[1,1536,2560]{2,1,0:T(8,128)(2,1)}) fusion(bf16[2,1536,2560]{2,1,0:T(8,128)(2,1)} %get-tuple-element.218, s32[]{:T(128)} %get-tuple-element.201, bf16[2,1536,2560]{2,1,0:T(8,128)(2,1)} %get-tuple-element.216), kind=kLoop, calls=%fused_computation.14.clone.1 | loop fusion | bytes 31457284 | tf_op jit(solution)/shard_map/while/body/jit(dynamic_index_in_dim)/dynamic_slice | solution.py:84
  555.0 10.6 %copy.70 = bf16[1,1536,2560]{1,2,0:T(8,128)(2,1)} copy(bf16[1,1536,2560]{2,1,0:T(8,128)(2,1)} %get-tuple-element.185) | data formatting | bytes 15728640 | tf_op jit(solution)/shard_map/while/body/jit(dynamic_index_in_dim)/dynamic_slice | solution.py:84
  565.6 1.3 dynamic-slice_bitcast_fusion.2
  566.9 20.6 %fusion.45 = (f32[20,384]{1,0:T(8,128)S(1)}, f32[20,1536,384]{2,1,0:T(8,128)}) fusion(pred[384,1536]{0,1:T(8,128)(4,1)S(1)} %dynamic-slice_bitcast_fusion.2, bf16[1536,20,128]{0,2,1:T(8,128)(2,1)} %bitcast.67, bf16[384,20,128]{2,0,1:T(8,128)(2,1)S(1)} %get-tuple-element.217), kind=kOutput, calls=%fused_computation.2.clone.1 | convolution fusion | flops 3055280640 | bytes 57636864 | tf_op jit(solution)/shard_map/while/body/eval_jaxpr/qhd,khd->hqk/dot_general | solution.py:26
  587.5 20.8 %fusion.46 = f32[20,384]{1,0:T(8,128)S(1)} fusion(f32[20,1536,384]{2,1,0:T(8,128)} %get-tuple-element.187, f32[20,384]{1,0:T(8,128)S(1)} %select_maximum_fusion.2, pred[384,1536]{0,1:T(8,128)(4,1)S(1)} %dynamic-slice_bitcast_fusion.2), kind=kLoop, calls=%fused_computation.4.clone.1 | loop fusion | flops 58974720 | bytes 47837184 | tf_op jit(solution)/shard_map/while/body/eval_jaxpr/reduce_sum | solution.py:33
  608.4 10.6 %copy.71 = bf16[1,1536,2560]{1,2,0:T(8,128)(2,1)} copy(bf16[1,1536,2560]{2,1,0:T(8,128)(2,1)} %get-tuple-element.189) | data formatting | bytes 15728640 | tf_op jit(solution)/shard_map/while/body/jit(dynamic_index_in_dim)/dynamic_slice | solution.py:84
  619.0 25.6 %fusion.48 = f32[20,384,128]{2,1,0:T(8,128)} fusion(f32[20,384,128]{2,1,0:T(8,128)} %get-tuple-element.204, bf16[1536,20,128]{0,2,1:T(8,128)(2,1)} %bitcast.68, f32[20,1536,384]{2,1,0:T(8,128)} %get-tuple-element.187, f32[20,384]{1,0:T(8,128)S(1)} %select_maximum_fusion.2, pred[384,1536]{0,1:T(8,128)(4,1)S(1)} %dynamic-slice_bitcast_fusion.2, ...), kind=kOutput, calls=%fused_computation.8.clone.1 | convolution fusion | flops 3081830400 | bytes 63565824 | tf_op jit(solution)/shard_map/while/body/eval_jaxpr/hqk,khd->hqd/dot_general | solution.py:34
  644.6 5.6 copy.51
  650.2 2.6 divide_convert_fusion
  652.7 17.0 %convolution_convert_fusion = bf16[384,5120]{1,0:T(8,128)(2,1)} fusion(bf16[384,2560]{0,1:T(8,128)(2,1)S(1)} %bitcast.77, bf16[2560,5120]{1,0:T(8,128)(2,1)} %param.17), kind=kOutput, calls=%fused_computation.26 | convolution fusion | flops 10068295680 | bytes 32112640 | tf_op jit(solution)/shard_map/dot_general | solution.py:90
  669.8 0.0 reduce-scatter.2.cloned.1.call-update
  669.8 3.0 copy.53
  672.8 4.1 copy.52
  676.8 4.4 copy.56
  681.2 4.1 multiply_reduce_fusion
  685.4 0.0 copy-start
  685.4 4.0 fusion.13
  689.4 0.0 copy-done
  689.4 4.3 fusion.19
  693.7 2.4 copy.57
  696.1 24.0 %reduce-scatter.2.cloned.1.call-done = bf16[384,2560]{1,0:T(8,128)(2,1)} async-done(((bf16[384,5120]{1,0:T(8,128)(2,1)}), bf16[384,2560]{1,0:T(8,128)(2,1)}) %reduce-scatter.2.cloned.1.call-update) | async-done | bytes 1966096 | tf_op jit(solution)/shard_map/reduce_scatter | solution.py:91
  (11 shorter events, 0.1 us)
Async XLA Ops:
  7.2 220.6 %all-gather.3.cloned.1.call-start = ((), (), s32[]{:S(2)}) async-start(), calls=%async_computation.1 | async-start | bytes 17694720 | tf_op jit(solution)/shard_map/all_gather | solution.py:66
  7.9 435.0 %all-gather.5.cloned.1.call-start = ((), (), s32[]{:S(2)}) async-start(), calls=%async_computation.2 | async-start | bytes 17694720 | tf_op jit(solution)/shard_map/all_gather | solution.py:67
  8.6 711.5 %reduce-scatter.2.cloned.1.call-start = ((), (), s32[]{:S(2)}) async-start(), calls=%async_computation.3 | async-start | bytes 5898240 | tf_op jit(solution)/shard_map/reduce_scatter | solution.py:91
  685.4 4.0 copy-start
Sparse Core Ops, SparseCore 0:
  10.2 217.4 all-gather.2
  229.9 212.9 all-gather.4
  669.9 50.1 reduce-scatter.1
where the time goes:
time: 729 us; the launch traced here: 727 us
  waiting for transfers between devices  451 us (62%)
  matrix products  117 us (16%)
  local copies, waits for them, and re-layouts  95.4 us (13%)
  other arithmetic  49.1 us (7%)
  between operations  13.9 us (2%)
    all_gather x1, waiting for transfers between devices, body(): value_piece = lax.all_gather(values, 'seq', axis=0, tiled=True)  215 us
    all_gather x1, waiting for transfers between devices, body(): key_piece = lax.all_gather(keys, 'seq', axis=0, tiled=True)  210 us
    dynamic_slice x6, local copies, waits for them, and re-layouts, body(): lax.scan(step, empty_state(heads_here, rows), (key_tiles, value_tiles, ma...  64.3 us
    dot_general x2, matrix products, attend_tile(): jnp.einsum('hqk,khd->hqd', weight.astype(jnp.bfloat16), value_three, pref...  50.5 us
    reduce_sum x2, other arithmetic, attend_tile(): total = total * factor + jnp.sum(weight, axis=2)  41.6 us
    dot_general x2, matrix products, attend_tile(): jnp.einsum('qhd,khd->hqk', query_three, key_three, preferred_element_type...  41.2 us
    reduce_scatter x1, waiting for transfers between devices, body(): lax.psum_scatter(term.astype(jnp.bfloat16), 'head', scatter_dimension=1,...  24 us
    unnamed x10, local copies, waits for them, and re-layouts  21.4 us
  transfers between devices with their start and end apart: 3, of which 3 were waited for; matrix products, arithmetic and copies ran while one was open for 5% of the time, Pallas kernels for 0%

commit v1 on v0

--- a/solution.py
+++ b/solution.py
@@ -1,6 +1,10 @@
+import functools
+
 import jax
 import jax.numpy as jnp
 from jax import lax
+from jax.experimental import pallas as pl
+from jax.experimental.pallas import tpu as pltpu
 from jax.sharding import PartitionSpec as P
 
 DH = 128
@@ -117,6 +121,276 @@
     return (block_stream, cross_heads)
 
 
+def fused_kernel(
+    sizes,
+    q_ref, k_ref, v_ref, cq_ref, tk_ref, tv_ref, w_ref, list_ref, count_ref,
+    out_ref, cross_ref,
+    kbuf, vbuf, qbuf, obuf, oin, wbuf, mine, ysend, yrecv, bias, cqb, tkb, tvb, cob,
+    kv_send, kv_recv, x_send, x_recv, q_send, q_recv, o_send, o_recv, y_send, y_recv, own_sem, own_q, own_o, c_sem, out_sem,
+):
+    nz, rows, group, text, slots = sizes
+    wide = group * DH
+    blocks = rows // BLK
+    chunk = nz * BLK
+    half = out_ref.shape[1]
+    seq = lax.axis_index("seq")
+    z, x = seq // 2, lax.rem(seq, 2)
+    y = lax.axis_index("head")
+    factor = (DH ** (-0.5)) * 1.4426950408889634
+
+    def at_z(zz):
+        return {"seq": zz * 2 + x}
+
+    def up(j):
+        return lax.rem(z + j, nz)
+
+    def down(j):
+        return lax.rem(z + nz - j, nz)
+
+    x_peer = {"seq": z * 2 + 1 - x}
+    y_peer = {"head": 1 - y}
+
+    def span(i, size):
+        return pl.ds(pl.multiple_of(i * size, size), size)
+
+    def remote(src, dst, send, recv, where):
+        return pltpu.make_async_remote_copy(
+            src_ref=src, dst_ref=dst, send_sem=send, recv_sem=recv,
+            device_id=where, device_id_type=pl.DeviceIdType.MESH,
+        )
+
+    def frame(zz, xx):
+        return span(zz * 2 + xx, rows)
+
+    own_w = pltpu.make_async_copy(w_ref, wbuf, own_sem.at[2])
+    own_w.start()
+
+    barrier = pltpu.get_barrier_semaphore()
+    for j in range(1, nz):
+        pl.semaphore_signal(barrier, inc=1, device_id=at_z(up(j)), device_id_type=pl.DeviceIdType.MESH)
+    pl.semaphore_signal(barrier, inc=1, device_id=x_peer, device_id_type=pl.DeviceIdType.MESH)
+    pl.semaphore_signal(barrier, inc=1, device_id=y_peer, device_id_type=pl.DeviceIdType.MESH)
+    pl.semaphore_wait(barrier, nz + 1)
+
+    pairs = ((k_ref, kbuf), (v_ref, vbuf))
+
+    def kv_copy(a, j):
+        return remote(pairs[a][0].at[:, span(up(j), wide)], pairs[a][1].at[frame(z, x), :],
+                      kv_send.at[a, j], kv_recv.at[a, j], at_z(up(j)))
+
+    def kv_landing(a, j):
+        place = pairs[a][1].at[frame(down(j), x), :]
+        return remote(place, place, kv_send.at[a, j], kv_recv.at[a, j], at_z(down(j)))
+
+    def x_copy(a, j):
+        place = pairs[a][1].at[frame(down(j), x), :]
+        source = place if j else pairs[a][0].at[:, span(z, wide)]
+        return remote(source, place, x_send.at[a, j], x_recv.at[a, j], x_peer)
+
+    def x_landing(a, j):
+        place = pairs[a][1].at[frame(down(j), 1 - x), :]
+        return remote(place, place, x_send.at[a, j], x_recv.at[a, j], x_peer)
+
+    def q_copy(c, j):
+        return remote(q_ref.at[span(c, BLK), span(up(j), wide)], qbuf.at[span(c * nz + z, BLK), :],
+                      q_send.at[c, j], q_recv.at[c, j], at_z(up(j)))
+
+    def q_landing(c, j):
+        place = qbuf.at[span(c * nz + down(j), BLK), :]
+        return remote(place, place, q_send.at[c, j], q_recv.at[c, j], at_z(down(j)))
+
+    def o_copy(c, j):
+        return remote(obuf.at[span(c * nz + up(j), BLK), :], oin.at[span(c, BLK), span(z, wide)],
+                      o_send.at[c, j], o_recv.at[c, j], at_z(up(j)))
+
+    def o_landing(c, j):
+        place = oin.at[span(c, BLK), span(down(j), wide)]
+        return remote(place, place, o_send.at[c, j], o_recv.at[c, j], at_z(down(j)))
+
+    def y_copy(c):
+        return remote(ysend.at[span(c, BLK), :], yrecv.at[span(c, BLK), :], y_send.at[c], y_recv.at[c], y_peer)
+
+    def own_kv(a):
+        return pltpu.make_async_copy(pairs[a][0].at[:, span(z, wide)], pairs[a][1].at[frame(z, x), :], own_sem.at[a])
+
+    def own_query(c):
+        return pltpu.make_async_copy(q_ref.at[span(c, BLK), span(z, wide)], qbuf.at[span(c * nz + z, BLK), :], own_q.at[c])
+
+    def own_out(c):
+        return pltpu.make_async_copy(obuf.at[span(c * nz + z, BLK), :], oin.at[span(c, BLK), span(z, wide)], own_o.at[c])
+
+    def out_copy(c):
+        return pltpu.make_async_copy(mine.at[span(c, BLK), :], out_ref.at[span(c, BLK), :], out_sem.at[c])
+
+    for a in range(2):
+        for j in range(nz - 1, 0, -1):
+            kv_copy(a, j).start()
+        x_copy(a, 0).start()
+        own_kv(a).start()
+    for c in range(blocks):
+        own_query(c).start()
+
+    key_block = lax.broadcasted_iota(jnp.int32, (1, bias.shape[1]), 1) // BLK
+
+    @pl.loop(0, blocks * nz)
+    def make_bias(i):
+        c, zz = i // nz, lax.rem(i, nz)
+        b = (zz * 2 + x) * blocks + c
+        used = count_ref[b]
+        line = jnp.full((1, bias.shape[1]), -1e30, jnp.float32)
+        for s in range(slots):
+            listed = jnp.where(s < used, list_ref[b, s], -1)
+            line = jnp.where(key_block == listed, 0.0, line)
+        bias[pl.ds(i, 1), :] = line
+
+    def attend(query, key, value, lines):
+        score = lax.dot_general(query, key, (((1,), (1,)), ((), ())), preferred_element_type=jnp.float32)
+        if lines is not None:
+            score = jnp.concatenate(
+                [score[i * BLK:(i + 1) * BLK] + line for i, line in enumerate(lines)], axis=0)
+        top = jnp.max(score, axis=1, keepdims=True)
+        weight = jnp.exp2((score - top) * factor)
+        total = jnp.sum(weight, axis=1, keepdims=True)
+        summed = jnp.dot(weight.astype(jnp.bfloat16), value, preferred_element_type=jnp.float32)
+        return (summed / total).astype(jnp.bfloat16)
+
+    @pl.loop(0, nz)
+    def cross(g):
+        cols = span(g, wide)
+        parts = [pltpu.make_async_copy(src.at[:, cols], dst, c_sem.at[n])
+                 for n, (src, dst) in enumerate(((cq_ref, cqb), (tk_ref, tkb), (tv_ref, tvb)))]
+        for part in parts:
+            part.start()
+        for part in parts:
+            part.wait()
+
+        @pl.loop(0, group)
+        def one(h):
+            head = span(h, DH)
+            cob[:, head] = attend(cqb[:, head], tkb[:, head], tvb[:, head], None)
+
+        back = pltpu.make_async_copy(cob, cross_ref.at[:, cols], c_sem.at[3])
+        back.start()
+        back.wait()
+
+    for j in range(1, nz):
+        kv_landing(0, j).wait_recv()
+        x_copy(0, j).start()
+    for c in range(blocks):
+        for j in range(nz - 1, 0, -1):
+            q_copy(c, j).start()
+    for j in range(1, nz):
+        kv_landing(1, j).wait_recv()
+        x_copy(1, j).start()
+    for a in range(2):
+        own_kv(a).wait()
+        for j in range(nz):
+            x_landing(a, j).wait_recv()
+    own_w.wait()
+
+    tile = 512
+
+    def project(c):
+        own_out(c).wait()
+        for j in range(1, nz):
+            o_landing(c, j).wait_recv()
+        here = span(c, BLK)
+
+        def part(base, into):
+            @pl.loop(0, half // tile)
+            def columns(n):
+                cols = pl.ds(pl.multiple_of(base * half + n * tile, tile), tile)
+                into[here, span(n, tile)] = jnp.dot(
+                    oin[here, :], wbuf[:, cols], preferred_element_type=jnp.float32).astype(jnp.bfloat16)
+
+        part(1 - y, ysend)
+        y_copy(c).start()
+        part(y, mine)
+
+    def finish(c):
+        y_copy(c).wait_recv()
+        here = span(c, BLK)
+        mine[here, :] = (mine[here, :].astype(jnp.float32) + yrecv[here, :].astype(jnp.float32)).astype(jnp.bfloat16)
+        out_copy(c).start()
+
+    @pl.loop(0, blocks)
+    def chunks(c):
+        own_query(c).wait()
+        for j in range(1, nz):
+            q_landing(c, j).wait_recv()
+
+        @pl.loop(0, group)
+        def one(h):
+            head = span(h, DH)
+            for r in range(nz // 2):
+                lines = [bias[pl.ds(c * nz + 2 * r + i, 1), :] for i in range(2)]
+                here = span(c * (nz // 2) + r, 2 * BLK)
+                obuf[here, head] = attend(qbuf[here, head], kbuf[:, head], vbuf[:, head], lines)
+
+        for j in range(nz - 1, 0, -1):
+            o_copy(c, j).start()
+        own_out(c).start()
+
+        @pl.when(c >= 1)
+        def earlier():
+            project(c - 1)
+
+    project(blocks - 1)
+    for c in range(blocks):
+        finish(c)
+    for c in range(blocks):
+        out_copy(c).wait()
+        y_copy(c).wait_send()
+        for j in range(1, nz):
+            q_copy(c, j).wait_send()
+            o_copy(c, j).wait_send()
+    for a in range(2):
+        for j in range(nz):
+            x_copy(a, j).wait_send()
+        for j in range(1, nz):
+            kv_copy(a, j).wait_send()
+
+
+def fused(nseq, queries, keys, values, cross_query, text_keys, text_values, out_weight, block_list, block_count):
+    nz = nseq // 2
+    rows, width = queries.shape
+    heads_here = width // DH
+    group = heads_here // nz
+    wide = group * DH
+    blocks = rows // BLK
+    tokens = nseq * rows
+    text = text_keys.shape[0]
+    half = out_weight.shape[1] // 2
+    bf = jnp.bfloat16
+    dma = pltpu.SemaphoreType.DMA
+    hbm = pl.BlockSpec(memory_space=pl.ANY)
+    smem = pl.BlockSpec(memory_space=pltpu.SMEM)
+    return pl.pallas_call(
+        functools.partial(fused_kernel, (nz, rows, group, text, block_list.shape[1])),
+        out_shape=(jax.ShapeDtypeStruct((rows, half), bf), jax.ShapeDtypeStruct((rows, width), bf)),
+        in_specs=[hbm] * 7 + [smem] * 2,
+        out_specs=(hbm, hbm),
+        scratch_shapes=[
+            pltpu.VMEM((tokens, wide), bf), pltpu.VMEM((tokens, wide), bf),
+            pltpu.VMEM((nz * rows, wide), bf), pltpu.VMEM((nz * rows, wide), bf),
+            pltpu.VMEM((rows, width), bf), pltpu.VMEM(out_weight.shape, bf),
+            pltpu.VMEM((rows, half), bf), pltpu.VMEM((rows, half), bf), pltpu.VMEM((rows, half), bf),
+            pltpu.VMEM((nz * blocks, tokens), jnp.float32),
+            pltpu.VMEM((rows, wide), bf), pltpu.VMEM((text, wide), bf), pltpu.VMEM((text, wide), bf),
+            pltpu.VMEM((rows, wide), bf),
+            dma((2, nz)), dma((2, nz)), dma((2, nz)), dma((2, nz)),
+            dma((blocks, nz)), dma((blocks, nz)), dma((blocks, nz)), dma((blocks, nz)),
+            dma((blocks,)), dma((blocks,)), dma((3,)), dma((blocks,)), dma((blocks,)), dma((4,)), dma((blocks,)),
+        ],
+        compiler_params=pltpu.CompilerParams(
+            collective_id=0, has_side_effects=True, vmem_limit_bytes=62 * 1024 * 1024),
+        cost_estimate=pl.CostEstimate(
+            flops=4 * rows * tokens * width + 4 * rows * width * half + 4 * rows * text * width,
+            bytes_accessed=2 * (6 * rows * width + 2 * text * width + 2 * width * half),
+            transcendentals=rows * heads_here * (tokens + text)),
+    )(queries, keys, values, cross_query, text_keys, text_values, out_weight, block_list, block_count)
+
+
 def solution(mesh):
     in_specs = (
         P(("pair", "seq"), "head"),
@@ -130,4 +404,12 @@
         P(),
     )
     out_specs = (P(("pair", "seq"), "head"), P(("pair", "seq"), "head"))
-    return jax.shard_map(body, mesh=mesh, in_specs=in_specs, out_specs=out_specs, check_vma=False)
+    nseq = mesh.shape["seq"]
+
+    def choose(*args):
+        width = args[0].shape[1]
+        nz = nseq // 2
+        fits = mesh.shape["head"] == 2 and nseq % 4 == 0 and (width // DH) % nz == 0
+        return functools.partial(fused, nseq)(*args) if fits else body(*args)
+
+    return jax.shard_map(choose, mesh=mesh, in_specs=in_specs, out_specs=out_specs, check_vma=False)

time: 729 us -> 228 us (0.31)
  waiting for transfers between devices: 451 us -> 0 us
  Pallas kernels: 0 us -> 221 us
  matrix products: 117 us -> 0 us
  local copies, waits for them, and re-layouts: 95.4 us -> 4.36 us
  other arithmetic: 49.1 us -> 0 us
  between operations: 13.9 us -> 0.65 us
    all_gather x2 -> x0, waiting for transfers between devices: 425 us -> none  [the longest x1 215 us: body(): value_piece = lax.all_gather(values, 'seq', axis=0, tiled=True)]
    pallas_call x0 -> x1, Pallas kernels: none -> 221 us  [fused(): pl.pallas_call(functools.partial(fused_kernel, (nz, rows, group, text, bl...]
    dot_general x7 -> x0, matrix products: 117 us -> none  [the longest x2 50.5 us: attend_tile(): jnp.einsum('hqk,khd->hqd', weight.astype(jnp.bfloat16), value_three, pref...]
    dynamic_slice x7 -> x0, local copies, waits for them, and re-layouts: 64.4 us -> none  [the longest x6 64.3 us: body(): lax.scan(step, empty_state(heads_here, rows), (key_tiles, value_tiles, ma...]
    reduce_sum x3 -> x0, other arithmetic: 45.6 us -> none  [the longest x2 41.6 us: attend_tile(): total = total * factor + jnp.sum(weight, axis=2)]
    reduce_scatter x1 -> x0, waiting for transfers between devices: 24 us -> none  [body(): lax.psum_scatter(term.astype(jnp.bfloat16), 'head', scatter_dimension=1,...]
    unnamed x10 -> x4, local copies, waits for them, and re-layouts: 21.4 us -> 4.36 us
  transfers between devices with their start and end apart: 3 -> 0, of which waited for: 3 -> 0; matrix products, arithmetic and copies ran while one was open for 5% -> 0% of each run, Pallas kernels for 0% -> 0%
where the time goes in v1:
time: 228 us; the launch traced here: 226 us
  Pallas kernels  221 us (97%)
  local copies, waits for them, and re-layouts  4.36 us (2%)
    pallas_call x1, Pallas kernels, fused(): pl.pallas_call(functools.partial(fused_kernel, (nz, rows, group, text, bl...  221 us

profile of v1, /device:TPU:0, one launch (start us, length us, event | category | flops | bytes accessed | tf_op | source)
XLA Modules:
  0.0 225.7 jit_solution(8580077784757115951)
XLA Ops:
  0.6 220.7 %shard_map.104 = (bf16[384,2560]{1,0:T(8,128)(2,1)}, bf16[384,2560]{1,0:T(8,128)(2,1)}) custom-call(bf16[384,2560]{1,0:T(8,128)(2,1)} %q_ref.1, bf16[384,2560]{1,0:T(8,128)(2,1)} %k_ref.1, bf16[384,2560]{1,0:T(8,128)(2,1)} %v_ref.1, bf16[384,2560]{1,0:T(8,128)(2,1)} %cq_ref.1, bf16[512,2560]{1,0:T(8,128)(2,1)} %tk_ref.1, bf16[512,2560]{1,0:T(8,128)(2,1)} %tv_ref.1, ...), custom_call_target="tpu_custom_call" | custom-call | flops 24159191040 | bytes 43253760 | tf_op jit(solution)/shard_map/pallas_call | solution.py:368
  221.3 0.0 copy-start
  221.3 3.1 %copy.13 = bf16[384,2560]{1,0:T(8,128)(2,1)} copy(bf16[384,2560]{1,0:T(8,128)(2,1)} %get-tuple-element.4) | data formatting | bytes 3932160
  224.4 0.0 copy-done
  224.4 1.3 copy.14
Async XLA Ops:
  221.3 3.1 %copy-start = (bf16[384,2560]{1,0:T(8,128)(2,1)S(1)}, bf16[384,2560]{1,0:T(8,128)(2,1)}, u32[]{:S(2)}) copy-start(bf16[384,2560]{1,0:T(8,128)(2,1)} %get-tuple-element.5) | copy-start | bytes 5898244

commit v2 on v1

--- a/solution.py
+++ b/solution.py
@@ -136,6 +136,7 @@
     seq = lax.axis_index("seq")
     z, x = seq // 2, lax.rem(seq, 2)
     y = lax.axis_index("head")
+    tile = 512
     factor = (DH ** (-0.5)) * 1.4426950408889634
 
     def at_z(zz):
@@ -173,23 +174,24 @@
     pl.semaphore_wait(barrier, nz + 1)
 
     pairs = ((k_ref, kbuf), (v_ref, vbuf))
-
-    def kv_copy(a, j):
-        return remote(pairs[a][0].at[:, span(up(j), wide)], pairs[a][1].at[frame(z, x), :],
-                      kv_send.at[a, j], kv_recv.at[a, j], at_z(up(j)))
-
-    def kv_landing(a, j):
-        place = pairs[a][1].at[frame(down(j), x), :]
-        return remote(place, place, kv_send.at[a, j], kv_recv.at[a, j], at_z(down(j)))
-
-    def x_copy(a, j):
-        place = pairs[a][1].at[frame(down(j), x), :]
-        source = place if j else pairs[a][0].at[:, span(z, wide)]
-        return remote(source, place, x_send.at[a, j], x_recv.at[a, j], x_peer)
-
-    def x_landing(a, j):
-        place = pairs[a][1].at[frame(down(j), 1 - x), :]
-        return remote(place, place, x_send.at[a, j], x_recv.at[a, j], x_peer)
+    early = blocks - 1
+
+    def kv_copy(a, h, j):
+        return remote(pairs[a][0].at[:, span(up(j) * group + h, DH)], pairs[a][1].at[frame(z, x), span(h, DH)],
+                      kv_send.at[a * group + h, j], kv_recv.at[a * group + h, j], at_z(up(j)))
+
+    def kv_landing(a, h, j):
+        place = pairs[a][1].at[frame(down(j), x), span(h, DH)]
+        return remote(place, place, kv_send.at[a * group + h, j], kv_recv.at[a * group + h, j], at_z(down(j)))
+
+    def x_copy(a, h, j):
+        place = pairs[a][1].at[frame(down(j), x), span(h, DH)]
+        source = place if j else pairs[a][0].at[:, span(z * group + h, DH)]
+        return remote(source, place, x_send.at[a * group + h, j], x_recv.at[a * group + h, j], x_peer)
+
+    def x_landing(a, h, j):
+        place = pairs[a][1].at[frame(down(j), 1 - x), span(h, DH)]
+        return remote(place, place, x_send.at[a * group + h, j], x_recv.at[a * group + h, j], x_peer)
 
     def q_copy(c, j):
         return remote(q_ref.at[span(c, BLK), span(up(j), wide)], qbuf.at[span(c * nz + z, BLK), :],
@@ -199,16 +201,17 @@
         place = qbuf.at[span(c * nz + down(j), BLK), :]
         return remote(place, place, q_send.at[c, j], q_recv.at[c, j], at_z(down(j)))
 
-    def o_copy(c, j):
-        return remote(obuf.at[span(c * nz + up(j), BLK), :], oin.at[span(c, BLK), span(z, wide)],
-                      o_send.at[c, j], o_recv.at[c, j], at_z(up(j)))
-
-    def o_landing(c, j):
-        place = oin.at[span(c, BLK), span(down(j), wide)]
-        return remote(place, place, o_send.at[c, j], o_recv.at[c, j], at_z(down(j)))
-
-    def y_copy(c):
-        return remote(ysend.at[span(c, BLK), :], yrecv.at[span(c, BLK), :], y_send.at[c], y_recv.at[c], y_peer)
+    def o_copy(c, h, j):
+        return remote(obuf.at[span(c * nz + up(j), BLK), span(h, DH)], oin.at[span(c, BLK), span(z * group + h, DH)],
+                      o_send.at[c * group + h, j], o_recv.at[c * group + h, j], at_z(up(j)))
+
+    def o_landing(c, h, j):
+        place = oin.at[span(c, BLK), span(down(j) * group + h, DH)]
+        return remote(place, place, o_send.at[c * group + h, j], o_recv.at[c * group + h, j], at_z(down(j)))
+
+    def y_copy(c, n):
+        return remote(ysend.at[span(c, BLK), span(n, tile)], yrecv.at[span(c, BLK), span(n, tile)],
+                      y_send.at[c, n], y_recv.at[c, n], y_peer)
 
     def own_kv(a):
         return pltpu.make_async_copy(pairs[a][0].at[:, span(z, wide)], pairs[a][1].at[frame(z, x), :], own_sem.at[a])
@@ -222,10 +225,22 @@
     def out_copy(c):
         return pltpu.make_async_copy(mine.at[span(c, BLK), :], out_ref.at[span(c, BLK), :], out_sem.at[c])
 
+    def send_queries(c):
+        for j in range(nz - 1, 0, -1):
+            q_copy(c, j).start()
+
+    def send_head(h):
+        for a in range(2):
+            for j in range(nz - 1, 0, -1):
+                kv_copy(a, h, j).start()
+            x_copy(a, h, 0).start()
+
+    send_queries(0)
+    send_head(0)
+    for c in range(1, early):
+        send_queries(c)
+    send_head(1)
     for a in range(2):
-        for j in range(nz - 1, 0, -1):
-            kv_copy(a, j).start()
-        x_copy(a, 0).start()
         own_kv(a).start()
     for c in range(blocks):
         own_query(c).start()
@@ -273,82 +288,142 @@
         back.start()
         back.wait()
 
-    for j in range(1, nz):
-        kv_landing(0, j).wait_recv()
-        x_copy(0, j).start()
-    for c in range(blocks):
-        for j in range(nz - 1, 0, -1):
-            q_copy(c, j).start()
-    for j in range(1, nz):
-        kv_landing(1, j).wait_recv()
-        x_copy(1, j).start()
-    for a in range(2):
-        own_kv(a).wait()
-        for j in range(nz):
-            x_landing(a, j).wait_recv()
-    own_w.wait()
-
-    tile = 512
-
-    def project(c):
-        own_out(c).wait()
-        for j in range(1, nz):
-            o_landing(c, j).wait_recv()
-        here = span(c, BLK)
-
-        def part(base, into):
-            @pl.loop(0, half // tile)
-            def columns(n):
-                cols = pl.ds(pl.multiple_of(base * half + n * tile, tile), tile)
-                into[here, span(n, tile)] = jnp.dot(
-                    oin[here, :], wbuf[:, cols], preferred_element_type=jnp.float32).astype(jnp.bfloat16)
-
-        part(1 - y, ysend)
-        y_copy(c).start()
-        part(y, mine)
-
-    def finish(c):
-        y_copy(c).wait_recv()
-        here = span(c, BLK)
-        mine[here, :] = (mine[here, :].astype(jnp.float32) + yrecv[here, :].astype(jnp.float32)).astype(jnp.bfloat16)
-        out_copy(c).start()
-
-    @pl.loop(0, blocks)
-    def chunks(c):
+    def attend_chunk(c, h):
+        head = span(h, DH)
+        for r in range(nz // 2):
+            lines = [bias[pl.ds(c * nz + 2 * r + i, 1), :] for i in range(2)]
+            here = span(c * (nz // 2) + r, 2 * BLK)
+            obuf[here, head] = attend(qbuf[here, head], kbuf[:, head], vbuf[:, head], lines)
+
+    def wait_queries(c):
         own_query(c).wait()
         for j in range(1, nz):
             q_landing(c, j).wait_recv()
 
+    def project(c):
+        own_out(c).wait()
+
+        @pl.loop(0, group)
+        def arrived(h):
+            for j in range(1, nz):
+                o_landing(c, h, j).wait_recv()
+
+        here = span(c, BLK)
+
+        def product(base, n):
+            cols = pl.ds(pl.multiple_of(base * half + n * tile, tile), tile)
+            return jnp.dot(oin[here, :], wbuf[:, cols], preferred_element_type=jnp.float32).astype(jnp.bfloat16)
+
+        @pl.loop(0, half // tile)
+        def theirs(n):
+            ysend[here, span(n, tile)] = product(1 - y, n)
+            y_copy(c, n).start()
+
+        @pl.loop(0, half // tile)
+        def ours(n):
+            mine[here, span(n, tile)] = product(y, n)
+
+    def finish(c):
+        here = span(c, BLK)
+
+        @pl.loop(0, half // tile)
+        def columns(n):
+            y_copy(c, n).wait_recv()
+            cols = span(n, tile)
+            mine[here, cols] = (mine[here, cols].astype(jnp.float32) + yrecv[here, cols].astype(jnp.float32)).astype(jnp.bfloat16)
+
+        out_copy(c).start()
+
+    for a in range(2):
+        own_kv(a).wait()
+
+    @pl.loop(0, group + 1)
+    def arrive(h):
+        @pl.when(h < group)
+        def pass_on():
+            for a in range(2):
+                for j in range(1, nz):
+                    kv_landing(a, h, j).wait_recv()
+                    x_copy(a, h, j).start()
+
+        @pl.when(h + 2 < group)
+        def more():
+            send_head(h + 2)
+
+        @pl.when(h == max(group - 2, 0))
+        def last_queries():
+            for c in range(early, blocks):
+                send_queries(c)
+
+        @pl.when(h == 1)
+        def first_queries():
+            for c in range(early):
+                wait_queries(c)
+
+        @pl.when(h >= 1)
+        def compute():
+            for a in range(2):
+                for j in range(nz):
+                    x_landing(a, h - 1, j).wait_recv()
+
+            @pl.loop(0, early)
+            def one(c):
+                attend_chunk(c, h - 1)
+
+    def send_outputs(c, h):
+        for j in range(nz - 1, 0, -1):
+            o_copy(c, h, j).start()
+
+    @pl.loop(0, early)
+    def give_back(c):
+        own_out(c).start()
+
         @pl.loop(0, group)
         def one(h):
-            head = span(h, DH)
-            for r in range(nz // 2):
-                lines = [bias[pl.ds(c * nz + 2 * r + i, 1), :] for i in range(2)]
-                here = span(c * (nz // 2) + r, 2 * BLK)
-                obuf[here, head] = attend(qbuf[here, head], kbuf[:, head], vbuf[:, head], lines)
-
-        for j in range(nz - 1, 0, -1):
-            o_copy(c, j).start()
+            send_outputs(c, h)
+
+    own_w.wait()
+    for c in range(early, blocks):
+        wait_queries(c)
+
+        @pl.loop(0, group)
+        def one(h):
+            attend_chunk(c, h)
+            send_outputs(c, h)
+
         own_out(c).start()
 
-        @pl.when(c >= 1)
-        def earlier():
-            project(c - 1)
-
-    project(blocks - 1)
-    for c in range(blocks):
+    @pl.loop(0, blocks)
+    def projected(c):
+        project(c)
+
+    @pl.loop(0, blocks)
+    def finished(c):
         finish(c)
-    for c in range(blocks):
+
+    @pl.loop(0, blocks)
+    def drained(c):
         out_copy(c).wait()
-        y_copy(c).wait_send()
+
+        @pl.loop(0, half // tile)
+        def one(n):
+            y_copy(c, n).wait_send()
+
+        @pl.loop(0, group)
+        def two(h):
+            for j in range(1, nz):
+                o_copy(c, h, j).wait_send()
+
         for j in range(1, nz):
             q_copy(c, j).wait_send()
-            o_copy(c, j).wait_send()
-    for a in range(2):
-        for j in range(nz):
-            x_copy(a, j).wait_send()
-        for j in range(1, nz):
-            kv_copy(a, j).wait_send()
+
+    @pl.loop(0, group)
+    def heads_sent(h):
+        for a in range(2):
+            for j in range(nz):
+                x_copy(a, h, j).wait_send()
+            for j in range(1, nz):
+                kv_copy(a, h, j).wait_send()
 
 
 def fused(nseq, queries, keys, values, cross_query, text_keys, text_values, out_weight, block_list, block_count):
@@ -378,9 +453,9 @@
             pltpu.VMEM((nz * blocks, tokens), jnp.float32),
             pltpu.VMEM((rows, wide), bf), pltpu.VMEM((text, wide), bf), pltpu.VMEM((text, wide), bf),
             pltpu.VMEM((rows, wide), bf),
-            dma((2, nz)), dma((2, nz)), dma((2, nz)), dma((2, nz)),
-            dma((blocks, nz)), dma((blocks, nz)), dma((blocks, nz)), dma((blocks, nz)),
-            dma((blocks,)), dma((blocks,)), dma((3,)), dma((blocks,)), dma((blocks,)), dma((4,)), dma((blocks,)),
+            dma((2 * group, nz)), dma((2 * group, nz)), dma((2 * group, nz)), dma((2 * group, nz)),
+            dma((blocks, nz)), dma((blocks, nz)), dma((blocks * group, nz)), dma((blocks * group, nz)),
+            dma((blocks, half // 512)), dma((blocks, half // 512)), dma((3,)), dma((blocks,)), dma((blocks,)), dma((4,)), dma((blocks,)),
         ],
         compiler_params=pltpu.CompilerParams(
             collective_id=0, has_side_effects=True, vmem_limit_bytes=62 * 1024 * 1024),
@@ -409,7 +484,7 @@
     def choose(*args):
         width = args[0].shape[1]
         nz = nseq // 2
-        fits = mesh.shape["head"] == 2 and nseq % 4 == 0 and (width // DH) % nz == 0
+        fits = mesh.shape["head"] == 2 and nseq % 4 == 0 and (width // DH) % nz == 0 and width // DH >= 2 * nz
         return functools.partial(fused, nseq)(*args) if fits else body(*args)
 
     return jax.shard_map(choose, mesh=mesh, in_specs=in_specs, out_specs=out_specs, check_vma=False)

time: 228 us -> 215 us (0.943); the launches traced: 226 us -> 215 us
  Pallas kernels: 221 us -> 210 us
    pallas_call x1, Pallas kernels: 221 us -> 210 us  [fused(): pl.pallas_call(functools.partial(fused_kernel, (nz, rows, group, text, bl...]
where the time goes in v2:
time: 215 us
  Pallas kernels  210 us (98%)
  local copies, waits for them, and re-layouts  4.36 us (2%)
    pallas_call x1, Pallas kernels, fused(): pl.pallas_call(functools.partial(fused_kernel, (nz, rows, group, text, bl...  210 us
    unnamed x4, local copies, waits for them, and re-layouts  4.36 us

profile of v2, /device:TPU:0, one launch (start us, length us, event | category | flops | bytes accessed | tf_op | source)
XLA Modules:
  0.0 215.2 jit_solution(10178112004747461586)
XLA Ops:
  0.6 210.2 %shard_map.104 = (bf16[384,2560]{1,0:T(8,128)(2,1)}, bf16[384,2560]{1,0:T(8,128)(2,1)}) custom-call(bf16[384,2560]{1,0:T(8,128)(2,1)} %q_ref.1, bf16[384,2560]{1,0:T(8,128)(2,1)} %k_ref.1, bf16[384,2560]{1,0:T(8,128)(2,1)} %v_ref.1, bf16[384,2560]{1,0:T(8,128)(2,1)} %cq_ref.1, bf16[512,2560]{1,0:T(8,128)(2,1)} %tk_ref.1, bf16[512,2560]{1,0:T(8,128)(2,1)} %tv_ref.1, ...), custom_call_target="tpu_custom_call" | custom-call | flops 24159191040 | bytes 43253760 | tf_op jit(solution)/shard_map/pallas_call | solution.py:443
  210.8 0.0 copy-start
  210.8 3.1 %copy.13 = bf16[384,2560]{1,0:T(8,128)(2,1)} copy(bf16[384,2560]{1,0:T(8,128)(2,1)} %get-tuple-element.4) | data formatting | bytes 3932160
  213.9 0.0 copy-done
  213.9 1.3 copy.14
Async XLA Ops:
  210.8 3.1 %copy-start = (bf16[384,2560]{1,0:T(8,128)(2,1)S(1)}, bf16[384,2560]{1,0:T(8,128)(2,1)}, u32[]{:S(2)}) copy-start(bf16[384,2560]{1,0:T(8,128)(2,1)} %get-tuple-element.5) | copy-start | bytes 5898244

commit v3 on v2

--- a/solution.py
+++ b/solution.py
@@ -193,41 +193,60 @@
         place = pairs[a][1].at[frame(down(j), 1 - x), span(h, DH)]
         return remote(place, place, x_send.at[a * group + h, j], x_recv.at[a * group + h, j], x_peer)
 
-    def q_copy(c, j):
-        return remote(q_ref.at[span(c, BLK), span(up(j), wide)], qbuf.at[span(c * nz + z, BLK), :],
-                      q_send.at[c, j], q_recv.at[c, j], at_z(up(j)))
-
-    def q_landing(c, j):
-        place = qbuf.at[span(c * nz + down(j), BLK), :]
-        return remote(place, place, q_send.at[c, j], q_recv.at[c, j], at_z(down(j)))
-
-    def o_copy(c, h, j):
-        return remote(obuf.at[span(c * nz + up(j), BLK), span(h, DH)], oin.at[span(c, BLK), span(z * group + h, DH)],
-                      o_send.at[c * group + h, j], o_recv.at[c * group + h, j], at_z(up(j)))
-
-    def o_landing(c, h, j):
-        place = oin.at[span(c, BLK), span(down(j) * group + h, DH)]
-        return remote(place, place, o_send.at[c * group + h, j], o_recv.at[c * group + h, j], at_z(down(j)))
-
-    def y_copy(c, n):
-        return remote(ysend.at[span(c, BLK), span(n, tile)], yrecv.at[span(c, BLK), span(n, tile)],
-                      y_send.at[c, n], y_recv.at[c, n], y_peer)
+    def part_of(unit, zz):
+        u, start, size = unit
+        return pl.ds(pl.multiple_of(start * nz + zz * size, size), size)
+
+    def rows_of(unit):
+        u, start, size = unit
+        return pl.ds(pl.multiple_of(start, size), size)
+
+    def q_copy(unit, j):
+        return remote(q_ref.at[rows_of(unit), span(up(j), wide)], qbuf.at[part_of(unit, z), :],
+                      q_send.at[unit[0], j], q_recv.at[unit[0], j], at_z(up(j)))
+
+    def q_landing(unit, j):
+        place = qbuf.at[part_of(unit, down(j)), :]
+        return remote(place, place, q_send.at[unit[0], j], q_recv.at[unit[0], j], at_z(down(j)))
+
+    def o_copy(unit, h, j):
+        mark = unit[0] * group + h
+        return remote(obuf.at[part_of(unit, up(j)), span(h, DH)], oin.at[rows_of(unit), span(z * group + h, DH)],
+                      o_send.at[mark, j], o_recv.at[mark, j], at_z(up(j)))
+
+    def o_landing(unit, h, j):
+        mark = unit[0] * group + h
+        place = oin.at[rows_of(unit), span(down(j) * group + h, DH)]
+        return remote(place, place, o_send.at[mark, j], o_recv.at[mark, j], at_z(down(j)))
+
+    def y_copy(unit, n):
+        here = rows_of(unit)
+        return remote(ysend.at[here, span(n, tile)], yrecv.at[here, span(n, tile)],
+                      y_send.at[unit[0], n], y_recv.at[unit[0], n], y_peer)
 
     def own_kv(a):
         return pltpu.make_async_copy(pairs[a][0].at[:, span(z, wide)], pairs[a][1].at[frame(z, x), :], own_sem.at[a])
 
-    def own_query(c):
-        return pltpu.make_async_copy(q_ref.at[span(c, BLK), span(z, wide)], qbuf.at[span(c * nz + z, BLK), :], own_q.at[c])
-
-    def own_out(c):
-        return pltpu.make_async_copy(obuf.at[span(c * nz + z, BLK), :], oin.at[span(c, BLK), span(z, wide)], own_o.at[c])
-
-    def out_copy(c):
-        return pltpu.make_async_copy(mine.at[span(c, BLK), :], out_ref.at[span(c, BLK), :], out_sem.at[c])
-
-    def send_queries(c):
+    def own_query(unit):
+        return pltpu.make_async_copy(q_ref.at[rows_of(unit), span(z, wide)], qbuf.at[part_of(unit, z), :], own_q.at[unit[0]])
+
+    def own_out(unit):
+        return pltpu.make_async_copy(obuf.at[part_of(unit, z), :], oin.at[rows_of(unit), span(z, wide)], own_o.at[unit[0]])
+
+    def out_copy(unit):
+        here = rows_of(unit)
+        return pltpu.make_async_copy(mine.at[here, :], out_ref.at[here, :], out_sem.at[unit[0]])
+
+    def early_unit(c):
+        return (c, c * BLK, BLK)
+
+    cut = BLK // 2
+    late = [(early + i, early * BLK + i * cut, cut) for i in range(2)]
+    units = [early_unit(c) for c in range(early)] + late
+
+    def send_queries(unit):
         for j in range(nz - 1, 0, -1):
-            q_copy(c, j).start()
+            q_copy(unit, j).start()
 
     def send_head(h):
         for a in range(2):
@@ -235,15 +254,15 @@
                 kv_copy(a, h, j).start()
             x_copy(a, h, 0).start()
 
-    send_queries(0)
+    send_queries(units[0])
     send_head(0)
     for c in range(1, early):
-        send_queries(c)
+        send_queries(units[c])
     send_head(1)
     for a in range(2):
         own_kv(a).start()
-    for c in range(blocks):
-        own_query(c).start()
+    for unit in units:
+        own_query(unit).start()
 
     key_block = lax.broadcasted_iota(jnp.int32, (1, bias.shape[1]), 1) // BLK
 
@@ -261,8 +280,9 @@
     def attend(query, key, value, lines):
         score = lax.dot_general(query, key, (((1,), (1,)), ((), ())), preferred_element_type=jnp.float32)
         if lines is not None:
+            step = score.shape[0] // len(lines)
             score = jnp.concatenate(
-                [score[i * BLK:(i + 1) * BLK] + line for i, line in enumerate(lines)], axis=0)
+                [score[i * step:(i + 1) * step] + line for i, line in enumerate(lines)], axis=0)
         top = jnp.max(score, axis=1, keepdims=True)
         weight = jnp.exp2((score - top) * factor)
         total = jnp.sum(weight, axis=1, keepdims=True)
@@ -288,27 +308,29 @@
         back.start()
         back.wait()
 
-    def attend_chunk(c, h):
+    def attend_chunk(unit, block, h):
+        u, start, size = unit
         head = span(h, DH)
-        for r in range(nz // 2):
-            lines = [bias[pl.ds(c * nz + 2 * r + i, 1), :] for i in range(2)]
-            here = span(c * (nz // 2) + r, 2 * BLK)
+        many = 2 * BLK // size
+        for r in range(nz // many):
+            lines = [bias[pl.ds(block * nz + many * r + i, 1), :] for i in range(many)]
+            here = pl.ds(pl.multiple_of(start * nz + r * 2 * BLK, 2 * BLK), 2 * BLK)
             obuf[here, head] = attend(qbuf[here, head], kbuf[:, head], vbuf[:, head], lines)
 
-    def wait_queries(c):
-        own_query(c).wait()
+    def wait_queries(unit):
+        own_query(unit).wait()
         for j in range(1, nz):
-            q_landing(c, j).wait_recv()
-
-    def project(c):
-        own_out(c).wait()
+            q_landing(unit, j).wait_recv()
+
+    def project(unit):
+        own_out(unit).wait()
 
         @pl.loop(0, group)
         def arrived(h):
             for j in range(1, nz):
-                o_landing(c, h, j).wait_recv()
-
-        here = span(c, BLK)
+                o_landing(unit, h, j).wait_recv()
+
+        here = rows_of(unit)
 
         def product(base, n):
             cols = pl.ds(pl.multiple_of(base * half + n * tile, tile), tile)
@@ -317,22 +339,22 @@
         @pl.loop(0, half // tile)
         def theirs(n):
             ysend[here, span(n, tile)] = product(1 - y, n)
-            y_copy(c, n).start()
+            y_copy(unit, n).start()
 
         @pl.loop(0, half // tile)
         def ours(n):
             mine[here, span(n, tile)] = product(y, n)
 
-    def finish(c):
-        here = span(c, BLK)
+    def finish(unit):
+        here = rows_of(unit)
 
         @pl.loop(0, half // tile)
         def columns(n):
-            y_copy(c, n).wait_recv()
+            y_copy(unit, n).wait_recv()
             cols = span(n, tile)
             mine[here, cols] = (mine[here, cols].astype(jnp.float32) + yrecv[here, cols].astype(jnp.float32)).astype(jnp.bfloat16)
 
-        out_copy(c).start()
+        out_copy(unit).start()
 
     for a in range(2):
         own_kv(a).wait()
@@ -352,13 +374,13 @@
 
         @pl.when(h == max(group - 2, 0))
         def last_queries():
-            for c in range(early, blocks):
-                send_queries(c)
+            for unit in late:
+                send_queries(unit)
 
         @pl.when(h == 1)
         def first_queries():
             for c in range(early):
-                wait_queries(c)
+                wait_queries(units[c])
 
         @pl.when(h >= 1)
         def compute():
@@ -368,54 +390,57 @@
 
             @pl.loop(0, early)
             def one(c):
-                attend_chunk(c, h - 1)
-
-    def send_outputs(c, h):
+                attend_chunk(early_unit(c), c, h - 1)
+
+    def send_outputs(unit, h):
         for j in range(nz - 1, 0, -1):
-            o_copy(c, h, j).start()
+            o_copy(unit, h, j).start()
 
     @pl.loop(0, early)
     def give_back(c):
-        own_out(c).start()
+        own_out(early_unit(c)).start()
 
         @pl.loop(0, group)
         def one(h):
-            send_outputs(c, h)
+            send_outputs(early_unit(c), h)
 
     own_w.wait()
-    for c in range(early, blocks):
-        wait_queries(c)
+    for i, unit in enumerate(late):
+        wait_queries(unit)
 
         @pl.loop(0, group)
         def one(h):
-            attend_chunk(c, h)
-            send_outputs(c, h)
-
-        own_out(c).start()
-
-    @pl.loop(0, blocks)
+            attend_chunk(unit, early, h)
+            send_outputs(unit, h)
+
+        own_out(unit).start()
+        if i == 0:
+            project(units[0])
+
+    @pl.loop(1, early)
     def projected(c):
-        project(c)
-
-    @pl.loop(0, blocks)
-    def finished(c):
-        finish(c)
-
-    @pl.loop(0, blocks)
-    def drained(c):
-        out_copy(c).wait()
+        project(early_unit(c))
+
+    for unit in late:
+        project(unit)
+
+    for unit in units:
+        finish(unit)
+
+    for unit in units:
+        out_copy(unit).wait()
 
         @pl.loop(0, half // tile)
         def one(n):
-            y_copy(c, n).wait_send()
+            y_copy(unit, n).wait_send()
 
         @pl.loop(0, group)
         def two(h):
             for j in range(1, nz):
-                o_copy(c, h, j).wait_send()
+                o_copy(unit, h, j).wait_send()
 
         for j in range(1, nz):
-            q_copy(c, j).wait_send()
+            q_copy(unit, j).wait_send()
 
     @pl.loop(0, group)
     def heads_sent(h):
@@ -433,6 +458,7 @@
     group = heads_here // nz
     wide = group * DH
     blocks = rows // BLK
+    units = blocks + 1
     tokens = nseq * rows
     text = text_keys.shape[0]
     half = out_weight.shape[1] // 2
@@ -454,8 +480,8 @@
             pltpu.VMEM((rows, wide), bf), pltpu.VMEM((text, wide), bf), pltpu.VMEM((text, wide), bf),
             pltpu.VMEM((rows, wide), bf),
             dma((2 * group, nz)), dma((2 * group, nz)), dma((2 * group, nz)), dma((2 * group, nz)),
-            dma((blocks, nz)), dma((blocks, nz)), dma((blocks * group, nz)), dma((blocks * group, nz)),
-            dma((blocks, half // 512)), dma((blocks, half // 512)), dma((3,)), dma((blocks,)), dma((blocks,)), dma((4,)), dma((blocks,)),
+            dma((units, nz)), dma((units, nz)), dma((units * group, nz)), dma((units * group, nz)),
+            dma((units, half // 512)), dma((units, half // 512)), dma((3,)), dma((units,)), dma((units,)), dma((4,)), dma((units,)),
         ],
         compiler_params=pltpu.CompilerParams(
             collective_id=0, has_side_effects=True, vmem_limit_bytes=62 * 1024 * 1024),

time: 215 us -> 217 us (level)
  no operation moved by 1% of the time
where the time goes in v3:
time: 217 us
  Pallas kernels  212 us (98%)
  local copies, waits for them, and re-layouts  4.36 us (2%)
    pallas_call x1, Pallas kernels, fused(): pl.pallas_call(functools.partial(fused_kernel, (nz, rows, group, text, bl...  212 us
    unnamed x4, local copies, waits for them, and re-layouts  4.36 us

profile of v3, /device:TPU:0, one launch (start us, length us, event | category | flops | bytes accessed | tf_op | source)
XLA Modules:
  0.0 216.7 jit_solution(7139224311467547358)
XLA Ops:
  0.6 211.6 %shard_map.104 = (bf16[384,2560]{1,0:T(8,128)(2,1)}, bf16[384,2560]{1,0:T(8,128)(2,1)}) custom-call(bf16[384,2560]{1,0:T(8,128)(2,1)} %q_ref.1, bf16[384,2560]{1,0:T(8,128)(2,1)} %k_ref.1, bf16[384,2560]{1,0:T(8,128)(2,1)} %v_ref.1, bf16[384,2560]{1,0:T(8,128)(2,1)} %cq_ref.1, bf16[512,2560]{1,0:T(8,128)(2,1)} %tk_ref.1, bf16[512,2560]{1,0:T(8,128)(2,1)} %tv_ref.1, ...), custom_call_target="tpu_custom_call" | custom-call | flops 24159191040 | bytes 43253760 | tf_op jit(solution)/shard_map/pallas_call | solution.py:469
  212.3 0.0 copy-start
  212.3 3.1 %copy.13 = bf16[384,2560]{1,0:T(8,128)(2,1)} copy(bf16[384,2560]{1,0:T(8,128)(2,1)} %get-tuple-element.4) | data formatting | bytes 3932160
  215.4 0.0 copy-done
  215.4 1.3 copy.14
Async XLA Ops:
  212.3 3.1 %copy-start = (bf16[384,2560]{1,0:T(8,128)(2,1)S(1)}, bf16[384,2560]{1,0:T(8,128)(2,1)}, u32[]{:S(2)}) copy-start(bf16[384,2560]{1,0:T(8,128)(2,1)} %get-tuple-element.5) | copy-start | bytes 5898244

commit v4 on v3

--- a/solution.py
+++ b/solution.py
@@ -359,12 +359,16 @@
     for a in range(2):
         own_kv(a).wait()
 
+    def send_outputs(unit, h):
+        for j in range(nz - 1, 0, -1):
+            o_copy(unit, h, j).start()
+
     @pl.loop(0, group + 1)
     def arrive(h):
         @pl.when(h < group)
         def pass_on():
             for a in range(2):
-                for j in range(1, nz):
+                for j in range(nz - 1, 0, -1):
                     kv_landing(a, h, j).wait_recv()
                     x_copy(a, h, j).start()
 
@@ -376,6 +380,12 @@
         def last_queries():
             for unit in late:
                 send_queries(unit)
+
+        @pl.when(h == group)
+        def first_outputs():
+            @pl.loop(0, group - 1)
+            def one(i):
+                send_outputs(units[0], i)
 
         @pl.when(h == 1)
         def first_queries():
@@ -392,15 +402,11 @@
             def one(c):
                 attend_chunk(early_unit(c), c, h - 1)
 
-    def send_outputs(unit, h):
-        for j in range(nz - 1, 0, -1):
-            o_copy(unit, h, j).start()
-
     @pl.loop(0, early)
     def give_back(c):
         own_out(early_unit(c)).start()
 
-        @pl.loop(0, group)
+        @pl.loop(jnp.where(c == 0, group - 1, 0), group)
         def one(h):
             send_outputs(early_unit(c), h)
 

time: 217 us -> 209 us (0.963)
  Pallas kernels: 212 us -> 204 us
    pallas_call x1, Pallas kernels: 212 us -> 204 us  [fused(): pl.pallas_call(functools.partial(fused_kernel, (nz, rows, group, text, bl...]
where the time goes in v4:
time: 209 us
  Pallas kernels  204 us (98%)
  local copies, waits for them, and re-layouts  4.36 us (2%)
    pallas_call x1, Pallas kernels, fused(): pl.pallas_call(functools.partial(fused_kernel, (nz, rows, group, text, bl...  204 us
    unnamed x4, local copies, waits for them, and re-layouts  4.36 us

profile of v4, /device:TPU:0, one launch (start us, length us, event | category | flops | bytes accessed | tf_op | source)
XLA Modules:
  0.0 209.0 jit_solution(9761799089971749444)
XLA Ops:
  0.6 204.0 %shard_map.104 = (bf16[384,2560]{1,0:T(8,128)(2,1)}, bf16[384,2560]{1,0:T(8,128)(2,1)}) custom-call(bf16[384,2560]{1,0:T(8,128)(2,1)} %q_ref.1, bf16[384,2560]{1,0:T(8,128)(2,1)} %k_ref.1, bf16[384,2560]{1,0:T(8,128)(2,1)} %v_ref.1, bf16[384,2560]{1,0:T(8,128)(2,1)} %cq_ref.1, bf16[512,2560]{1,0:T(8,128)(2,1)} %tk_ref.1, bf16[512,2560]{1,0:T(8,128)(2,1)} %tv_ref.1, ...), custom_call_target="tpu_custom_call" | custom-call | flops 24159191040 | bytes 43253760 | tf_op jit(solution)/shard_map/pallas_call | solution.py:475
  204.6 0.0 copy-start
  204.7 3.1 %copy.13 = bf16[384,2560]{1,0:T(8,128)(2,1)} copy(bf16[384,2560]{1,0:T(8,128)(2,1)} %get-tuple-element.4) | data formatting | bytes 3932160
  207.7 0.0 copy-done
  207.7 1.3 copy.14
Async XLA Ops:
  204.6 3.1 %copy-start = (bf16[384,2560]{1,0:T(8,128)(2,1)S(1)}, bf16[384,2560]{1,0:T(8,128)(2,1)}, u32[]{:S(2)}) copy-start(bf16[384,2560]{1,0:T(8,128)(2,1)} %get-tuple-element.5) | copy-start | bytes 5898244

commit v5 on v4

--- a/solution.py
+++ b/solution.py
@@ -402,13 +402,13 @@
             def one(c):
                 attend_chunk(early_unit(c), c, h - 1)
 
-    @pl.loop(0, early)
-    def give_back(c):
-        own_out(early_unit(c)).start()
-
-        @pl.loop(jnp.where(c == 0, group - 1, 0), group)
-        def one(h):
-            send_outputs(early_unit(c), h)
+                @pl.when(h == group)
+                def give_back():
+                    own_out(early_unit(c)).start()
+
+                    @pl.loop(jnp.where(c == 0, group - 1, 0), group)
+                    def each(i):
+                        send_outputs(early_unit(c), i)
 
     own_w.wait()
     for i, unit in enumerate(late):

time: 209 us -> 209 us (level)
  no operation moved by 1% of the time
where the time goes in v5:
time: 209 us
  Pallas kernels  204 us (98%)
  local copies, waits for them, and re-layouts  4.36 us (2%)
    pallas_call x1, Pallas kernels, fused(): pl.pallas_call(functools.partial(fused_kernel, (nz, rows, group, text, bl...  204 us
    unnamed x4, local copies, waits for them, and re-layouts  4.36 us

profile of v5, /device:TPU:0, one launch (start us, length us, event | category | flops | bytes accessed | tf_op | source)
XLA Modules:
  0.0 209.0 jit_solution(6588653712229439354)
XLA Ops:
  0.6 204.0 %shard_map.104 = (bf16[384,2560]{1,0:T(8,128)(2,1)}, bf16[384,2560]{1,0:T(8,128)(2,1)}) custom-call(bf16[384,2560]{1,0:T(8,128)(2,1)} %q_ref.1, bf16[384,2560]{1,0:T(8,128)(2,1)} %k_ref.1, bf16[384,2560]{1,0:T(8,128)(2,1)} %v_ref.1, bf16[384,2560]{1,0:T(8,128)(2,1)} %cq_ref.1, bf16[512,2560]{1,0:T(8,128)(2,1)} %tk_ref.1, bf16[512,2560]{1,0:T(8,128)(2,1)} %tv_ref.1, ...), custom_call_target="tpu_custom_call" | custom-call | flops 24159191040 | bytes 43253760 | tf_op jit(solution)/shard_map/pallas_call | solution.py:475
  204.7 0.0 copy-start
  204.7 3.1 %copy.13 = bf16[384,2560]{1,0:T(8,128)(2,1)} copy(bf16[384,2560]{1,0:T(8,128)(2,1)} %get-tuple-element.4) | data formatting | bytes 3932160
  207.8 0.0 copy-done
  207.8 1.3 copy.14
Async XLA Ops:
  204.7 3.1 %copy-start = (bf16[384,2560]{1,0:T(8,128)(2,1)S(1)}, bf16[384,2560]{1,0:T(8,128)(2,1)}, u32[]{:S(2)}) copy-start(bf16[384,2560]{1,0:T(8,128)(2,1)} %get-tuple-element.5) | copy-start | bytes 5898244
